TPU v7x, 32 devices: a whole 2x2x4 slice. The times are simulated.
32 devices in a mesh: view: 4 (over y, x), joined: 8 (over z, core).
Axes of the slice: x: 2, y: 2, z: 4, core: 2. Of those that a mesh axis runs over, the one named last changes fastest.
Arguments:
- observed: float32 [4, 256, 16, 16, 128], P('view', 'joined'), may hold values from 0.25 to 4
- estimate: float32 [256, 16, 16, 128], P('joined'), may hold values from 0.5 to 2
- psf_taps: float32 [4, 3, 31], P('view'), may hold values from 0.02 to 1
- tile_block: int32 [4, 256], replicated, may hold values from 0 to 255, as said below
- weight_level: int32 [4, 256], P('view', 'joined'), may hold values from 0 to 7
Outputs:
- refined: float32 [256, 16, 16, 128], P('joined')
Inputs may be any that keep to these rules, and one draw needn't show every extreme that they name: `tile_block`: for each view the list names every one of the 256 blocks exactly once. Block b belongs to index b // 32 of joined; the tiles of one device are the aligned runs of 32 entries. Of one device's tiles of one view at most 8 lie in blocks of one owner, and in every view each device has an owner that gets exactly 8 of them.
All inputs are finite; a program needn't handle non-finite values.
Results may differ from a plain program's by a relative error of at most 0.0001.
Values sent between devices are 32-bit elements; how exact they have to be, the bound alone decides.
A program may use at most 128 MiB of HBM per device.

v0:
```python
import jax
import jax.numpy as jnp
from jax import lax
from jax.sharding import PartitionSpec as P


def band(kernel_row, extent):
    half_span = kernel_row.shape[0] // 2
    offset = jnp.arange(extent)[None, :] - jnp.arange(extent)[:, None] + half_span
    chosen = (offset[:, :, None] == jnp.arange(kernel_row.shape[0])[None, None, :]).astype(
        jnp.float32
    )
    return jnp.sum(chosen * kernel_row[None, None, :], axis=-1)


def shifted(volume, kernel_row, flipped):
    tap_count = kernel_row.shape[0]
    half_span = tap_count // 2
    extent_x = volume.shape[3]
    padded = jnp.pad(volume, ((0, 0), (0, 0), (0, 0), (half_span, half_span)))
    summed = jnp.zeros_like(volume)
    for tap_index in range(tap_count):
        begin = 2 * half_span - tap_index if flipped else tap_index
        summed = summed + kernel_row[tap_index] * padded[:, :, :, begin : begin + extent_x]
    return summed


def blur(volume, kernel_set):
    along_z = band(kernel_set[0], volume.shape[1])
    along_y = band(kernel_set[1], volume.shape[2])
    volume = jnp.einsum("az,tzyx->tayx", along_z, volume, precision=lax.Precision.HIGHEST)
    volume = jnp.einsum("by,tzyx->tzbx", along_y, volume, precision=lax.Precision.HIGHEST)
    return shifted(volume, kernel_set[2], False)


def spread(volume, kernel_set):
    along_z = band(kernel_set[0], volume.shape[1])
    along_y = band(kernel_set[1], volume.shape[2])
    volume = shifted(volume, kernel_set[2], True)
    volume = jnp.einsum("yb,tzyx->tzbx", along_y, volume, precision=lax.Precision.HIGHEST)
    return jnp.einsum("za,tzyx->tayx", along_z, volume, precision=lax.Precision.HIGHEST)


def shards(observed, estimate, psf_taps, tile_block, weight_level):
    kernel_set = psf_taps[0] / jnp.sum(psf_taps[0], axis=-1, keepdims=True)
    seen_tiles = observed[0]
    tile_weight = (weight_level[0].astype(jnp.float32) + 1.0) / 8.0
    owner_count = lax.axis_size("joined")
    joined_here = lax.axis_index("joined")
    view_here = lax.axis_index("view")
    tiles_dev = estimate.shape[0]
    slot_count = 2 * tiles_dev // owner_count
    all_slots = owner_count * slot_count
    listing = lax.dynamic_index_in_dim(tile_block, view_here, 0, keepdims=False)
    owners = listing // tiles_dev
    owner_grid = owners.reshape(owner_count, tiles_dev)
    earlier = jnp.arange(tiles_dev)[None, :] < jnp.arange(tiles_dev)[:, None]
    matching = owner_grid[:, :, None] == owner_grid[:, None, :]
    rank_list = jnp.sum((matching & earlier[None]).astype(jnp.int32), axis=2).reshape(-1)
    source = jnp.arange(listing.shape[0], dtype=jnp.int32) // tiles_dev
    is_mine = owners == joined_here
    local_block = listing - joined_here * tiles_dev
    source_slot = source * slot_count + rank_list
    outgoing = (
        jnp.full((all_slots,), tiles_dev, jnp.int32)
        .at[jnp.where(is_mine, source_slot, all_slots)]
        .set(local_block, mode="drop")
    )
    arrival = (
        jnp.zeros((tiles_dev,), jnp.int32)
        .at[jnp.where(is_mine, local_block, tiles_dev)]
        .set(source_slot, mode="drop")
    )
    my_slots = lax.dynamic_slice_in_dim(
        owners * slot_count + rank_list, joined_here * tiles_dev, tiles_dev
    )
    returning = (
        jnp.full((all_slots,), tiles_dev, jnp.int32)
        .at[my_slots]
        .set(jnp.arange(tiles_dev, dtype=jnp.int32))
    )

    def pack(values, table):
        picked = jnp.take(values, table, axis=0, mode="fill", fill_value=0.0)
        return picked.reshape((owner_count, slot_count) + values.shape[1:])

    def unpack(values, table):
        return jnp.take(values.reshape((all_slots,) + values.shape[2:]), table, axis=0)

    sending = pack(estimate, outgoing)
    arrived = lax.all_to_all(sending, "joined", split_axis=0, concat_axis=0, tiled=True)
    local_blocks = jnp.take(arrived.reshape((all_slots,) + estimate.shape[1:]), my_slots, axis=0)
    ratio_field = seen_tiles / blur(local_blocks, kernel_set)
    weighted = spread(ratio_field, kernel_set) * tile_weight[:, None, None, None]
    got_back = lax.all_to_all(
        pack(weighted, returning), "joined", split_axis=0, concat_axis=0, tiled=True
    )
    got_weight = lax.all_to_all(
        pack(tile_weight, returning), "joined", split_axis=0, concat_axis=0, tiled=True
    )
    num_total, den_total = lax.psum(
        (unpack(got_back, arrival), unpack(got_weight, arrival)), "view"
    )
    return estimate * (num_total / den_total[:, None, None, None])


def solution(mesh):
    return jax.shard_map(
        shards,
        mesh=mesh,
        in_specs=(
            P("view", "joined", None, None, None),
            P("joined", None, None, None),
            P("view", None, None),
            P(),
            P("view", "joined"),
        ),
        out_specs=P("joined", None, None, None),
        check_vma=False,
    )
```

profile of v0, /device:TPU:0, one launch (start us, length us, event | category | flops | bytes accessed | tf_op | source)
XLA Modules:
  0.0 700.3 jit_solution(10519103204371374091)
XLA Ops:
  6.5 0.7 compare_select_fusion
  7.8 0.7 reduce.7
  9.0 1.4 scatter_custom_fusion
  10.5 6.5 gather_fusion.2
  16.9 8.3 %broadcast_select_fusion.1 = f32[64,16,16,128]{3,2,1,0:T(8,128)} fusion(f32[64,16,16,128]{3,2,1,0:T(8,128)} %gather_fusion.2, pred[64]{0:T(512)(128)(4,1)S(1)} %compare_and_fusion.3), kind=kLoop, calls=%fused_computation.198 | loop fusion | flops 2097152 | bytes 16777280 | tf_op jit(solution)/shard_map/jit(_take)/select_n | solution.py:84
  25.2 6.5 all-to-all-start
  31.8 0.7 scatter_custom_fusion.1
  32.5 0.8 gather_fusion
  33.3 0.7 select_n.147
  34.2 0.7 fusion.197
  34.9 0.7 fusion.196
  35.8 179.9 %all-to-all-done = f32[8,8,16,16,128]{4,3,2,1,0:T(8,128)} async-done(((f32[8,8,16,16,128]{4,3,2,1,0:T(8,128)}), f32[8,8,16,16,128]{4,3,2,1,0:T(8,128)}, u32[]{:S(2)}, u32[]{:S(2)}) %all-to-all-start) | async-done | bytes 8388640 | tf_op jit(solution)/shard_map/all_to_all | solution.py:91
  215.7 3.4 all-to-all-start.2
  219.1 6.2 gather_fusion.3
  225.3 2.7 broadcast_select_fusion.3
  228.0 5.0 fusion.137
  233.1 5.0 fusion.140
  238.1 52.6 %fusion.53 = f32[32,16,16,128]{3,2,1,0:T(8,128)S(1)} fusion(f32[32,16,16,128]{3,2,1,0:T(8,128)S(1)} %fusion.140, f32[1,32,16,16,128]{4,3,2,1,0:T(8,128)S(1)} %copy-done, f32[]{:T(128)} %bitcast.45, f32[]{:T(128)} %bitcast.44, f32[]{:T(128)} %bitcast.43, f32[]{:T(128)} %bitcast.42, f32[]{:T(128)} %bitcast.41, f32[]{:T(128)} %bitcast.40, f32[]{:T(128)} %bitcast.39, ...), kind=kLoop, calls=%fused_computation.122 | loop fusion | flops 65011712 | bytes 12583036 | tf_op jit(solution)/shard_map/div | solution.py:93
  290.8 59.2 %fusion.145 = f32[32,16,16,128]{3,2,1,0:T(8,128)} fusion(f32[32,16,16,128]{3,2,1,0:T(8,128)S(1)} %fusion.53, f32[]{:T(128)} %bitcast.45, f32[]{:T(128)} %bitcast.44, f32[]{:T(128)} %bitcast.43, f32[]{:T(128)} %bitcast.42, f32[]{:T(128)} %bitcast.41, f32[]{:T(128)} %bitcast.40, f32[]{:T(128)} %bitcast.39, f32[]{:T(128)} %bitcast.38, f32[]{:T(128)} %bitcast.37, ...), kind=kOutput, calls=%fused_computation.203 | convolution fusion | flops 265289728 | bytes 8389756 | tf_op jit(solution)/shard_map/yb,tzyx->tzbx/dot_general | solution.py:40
  350.0 8.8 %multiply_bitcast_fusion = f32[32,16,16,128]{3,1,2,0:T(8,128)} fusion(f32[32,16,16,128]{3,2,1,0:T(8,128)} %fusion.145, f32[32]{0:T(128)S(1)} %multiply_bitcast_fusion.1, f32[16,16]{1,0:T(8,128)S(1)} %get-tuple-element.8), kind=kOutput, calls=%fused_computation.200 | convolution fusion | flops 202375168 | bytes 8389760 | tf_op jit(solution)/shard_map/za,tzyx->tayx/dot_general | solution.py:41
  358.7 6.5 gather_fusion.4
  365.2 8.3 %broadcast_select_fusion = f32[64,16,16,128]{3,1,2,0:T(8,128)} fusion(f32[64,16,16,128]{3,1,2,0:T(8,128)} %gather_fusion.4, pred[64]{0:T(512)(128)(4,1)S(1)} %get-tuple-element.12), kind=kLoop, calls=%fused_computation.197 | loop fusion | flops 2097152 | bytes 16777280 | tf_op jit(solution)/shard_map/jit(_take)/select_n | solution.py:84
  373.5 5.0 all-to-all-start.1
  378.5 1.7 scatter_custom_fusion.2
  381.5 0.7 gather_fusion.1
  382.2 180.1 %all-to-all-done.1 = f32[8,8,16,16,128]{4,2,3,1,0:T(8,128)} async-done(((f32[8,8,16,16,128]{4,2,3,1,0:T(8,128)}), f32[8,8,16,16,128]{4,2,3,1,0:T(8,128)}, u32[]{:S(2)}, u32[]{:S(2)}) %all-to-all-start.1) | async-done | bytes 8388640 | tf_op jit(solution)/shard_map/all_to_all | solution.py:95
  562.4 10.5 %copy.25 = f32[8,8,16,16,128]{4,3,2,1,0:T(8,128)} copy(f32[8,8,16,16,128]{4,2,3,1,0:T(8,128)} %all-to-all-done.1) | data formatting | bytes 16777216 | tf_op jit(solution)/shard_map/all_to_all | solution.py:95
  572.8 6.2 gather_fusion.5
  579.1 4.8 broadcast_select_fusion.2
  583.9 10.1 %psum.15 = f32[32]{0:T(128)S(1)} all-reduce(f32[32]{0:T(128)S(1)} %get-tuple-element.9), channel_id=1, replica_groups=mesh['view'=4,'joined'=8] {'view'}, use_global_device_ids=true, to_apply=%region_8.11 | all-reduce | flops 32 | bytes 256 | tf_op jit(solution)/shard_map/psum | solution.py:101
  594.0 92.8 %all-reduce.4.cloned.1.call-done = f32[32,16,16,128]{3,2,1,0:T(8,128)} async-done(((f32[32,16,16,128]{3,2,1,0:T(8,128)}), f32[32,16,16,128]{3,2,1,0:T(8,128)}) %all-reduce.4.cloned.1.call-update) | async-done | bytes 4194320 | tf_op jit(solution)/shard_map/psum | solution.py:101
  686.8 6.6 divide_multiply_fusion
  (39 shorter events, 3.0 us)
Async XLA Ops:
  25.2 7.3 %copy-start.2 = (s32[1,32]{1,0:T(1,128)S(1)}, s32[1,32]{1,0:T(1,128)}, u32[]{:S(2)}) copy-start(s32[1,32]{1,0:T(1,128)} %param.13) | copy-start | bytes 388
  25.2 8.7 %copy-start.1 = (f32[1,3,31]{2,0,1:T(1,128)S(1)}, f32[1,3,31]{2,0,1:T(1,128)}, u32[]{:S(2)}) copy-start(f32[1,3,31]{2,0,1:T(1,128)} %param.11) | copy-start | bytes 1120
  25.2 190.5 %all-to-all-start = ((f32[8,8,16,16,128]{4,3,2,1,0:T(8,128)}), f32[8,8,16,16,128]{4,3,2,1,0:T(8,128)}, u32[]{:S(2)}, u32[]{:S(2)}) async-start(f32[8,8,16,16,128]{4,3,2,1,0:T(8,128)} %bitcast.87), calls=%async_computation | async-start | bytes 16777216 | tf_op jit(solution)/shard_map/all_to_all | solution.py:91
  215.7 157.8 %all-to-all-start.2 = ((f32[8,1,8]{2,1,0:T(1,128)}), f32[8,1,8]{2,1,0:T(1,128)S(1)}, u32[]{:S(2)}, u32[]{:S(2)}) async-start(f32[8,1,8]{2,1,0:T(1,128)} %bitcast.53), calls=%async_computation.2 | async-start | bytes 8192 | tf_op jit(solution)/shard_map/all_to_all | solution.py:98
  233.1 5.1 copy-start
  373.5 188.9 %all-to-all-start.1 = ((f32[8,8,16,16,128]{4,2,3,1,0:T(8,128)}), f32[8,8,16,16,128]{4,2,3,1,0:T(8,128)}, u32[]{:S(2)}, u32[]{:S(2)}) async-start(f32[8,8,16,16,128]{4,2,3,1,0:T(8,128)} %bitcast.88), calls=%async_computation.1 | async-start | bytes 16777216 | tf_op jit(solution)/shard_map/all_to_all | solution.py:95
  378.5 308.3 %all-reduce.4.cloned.1.call-start = ((), (), s32[]{:S(2)}) async-start(), calls=%async_computation.3 | async-start | bytes 8388608 | tf_op jit(solution)/shard_map/psum | solution.py:101
Sparse Core Ops, SparseCore 0:
  584.0 102.7 all-reduce.3
where the time goes:
time: 702 us; the launch traced here: 700 us
  waiting for transfers between devices  453 us (65%)
  other arithmetic  86.2 us (12%)
  matrix products  78.1 us (11%)
  local copies, waits for them, and re-layouts  44.6 us (6%)
  starting transfers between devices  14.9 us (2%)
  between operations  13.6 us (2%)
  blocking collectives  10.1 us (1%)
    all_to_all x1, waiting for transfers between devices, shards(): lax.all_to_all(pack(weighted, returning), 'joined', split_axis=0, concat_...  180 us
    all_to_all x1, waiting for transfers between devices, shards(): lax.all_to_all(sending, 'joined', split_axis=0, concat_axis=0, tiled=True)  180 us
    psum x1, waiting for transfers between devices, shards(): lax.psum((unpack(got_back, arrival), unpack(got_weight, arrival)), 'view')  92.8 us
    dot_general x1, matrix products, spread(): jnp.einsum('yb,tzyx->tzbx', along_y, volume, precision=lax.Precision.HIGH...  59.2 us
    div x1, other arithmetic, shards(): ratio_field = seen_tiles / blur(local_blocks, kernel_set)  52.6 us
    select_n x5, other arithmetic, pack(): picked = jnp.take(values, table, axis=0, mode='fill', fill_value=0.0)  16.6 us
  transfers between devices with their start and end apart: 4, of which 3 were waited for; matrix products, arithmetic and copies ran while one was open for 23% of the time, Pallas kernels for 0%

commit v1 on v0

v1 whole, which is shorter than its diff:
```python
import functools

import jax
import jax.numpy as jnp
from jax import lax
from jax.experimental import pallas as pl
from jax.experimental.pallas import tpu as pltpu
from jax.sharding import PartitionSpec as P


def bands(rows, extent):
    taps = rows.shape[-1]
    offset = jnp.arange(extent)[None, :] - jnp.arange(extent)[:, None] + taps // 2
    chosen = (offset[:, :, None] == jnp.arange(taps)[None, None, :]).astype(jnp.float32)
    return jnp.sum(chosen * rows, axis=-1)


def split(value):
    high = value.astype(jnp.bfloat16)
    low = (value - high.astype(jnp.float32)).astype(jnp.bfloat16)
    return high, low


def matmul(a, b):
    dot = functools.partial(jnp.dot, preferred_element_type=jnp.float32)
    return dot(a[0], b[0]) + (dot(a[0], b[1]) + dot(a[1], b[0]))


def project_kernel(slot_ref, plane_ref, back_ref, line_ref, lineback_ref, weight_ref, seen_ref, estimate_ref, out_ref):
    block = pl.program_id(0)
    current = estimate_ref[0]
    blurred = matmul(split(matmul(split(plane_ref[...]), split(current))), split(lineback_ref[...]))
    ratio = seen_ref[0] / blurred
    spread = matmul(split(matmul(split(back_ref[...]), split(ratio))), split(line_ref[...]))
    out_ref[0] = weight_ref[block] * spread


def project(slot, plane, line, weight, seen, estimate):
    blocks, rows, lanes = estimate.shape
    whole = lambda array: pl.BlockSpec(array.shape, lambda i, slot: (0,) * array.ndim)
    return pl.pallas_call(
        project_kernel,
        grid_spec=pltpu.PrefetchScalarGridSpec(
            num_scalar_prefetch=1,
            grid=(blocks,),
            in_specs=[
                whole(plane),
                whole(plane),
                whole(line),
                whole(line),
                pl.BlockSpec(memory_space=pltpu.SMEM),
                pl.BlockSpec((1, rows, lanes), lambda i, slot: (slot[i], 0, 0)),
                pl.BlockSpec((1, rows, lanes), lambda i, slot: (i, 0, 0)),
            ],
            out_specs=pl.BlockSpec((1, rows, lanes), lambda i, slot: (i, 0, 0)),
        ),
        out_shape=jax.ShapeDtypeStruct(estimate.shape, jnp.float32),
        compiler_params=pltpu.CompilerParams(vmem_limit_bytes=32 * 1024 * 1024),
    )(slot, plane, plane.T, line, line.T, weight, seen, estimate)


def shards(observed, estimate, psf_taps, tile_block, weight_level):
    owner_count = lax.axis_size("joined")
    view_here, joined_here = lax.axis_index("view"), lax.axis_index("joined")
    tiles_dev, size_z, size_y, size_x = estimate.shape
    rows = size_z * size_y
    slot_count = 2 * tiles_dev // owner_count
    all_slots = owner_count * slot_count

    kernel_rows = psf_taps[0] / jnp.sum(psf_taps[0], axis=-1, keepdims=True)
    along_z = bands(kernel_rows[0], size_z)
    along_y = bands(kernel_rows[1], size_y)
    line = bands(kernel_rows[2], size_x)
    plane = (along_z[:, None, :, None] * along_y[None, :, None, :]).reshape(rows, rows)

    listing = lax.dynamic_index_in_dim(tile_block, view_here, 0, keepdims=False)
    owners = (listing // tiles_dev).reshape(owner_count, tiles_dev)
    earlier = jnp.arange(tiles_dev)[None, :] < jnp.arange(tiles_dev)[:, None]
    matching = owners[:, :, None] == owners[:, None, :]
    rank = jnp.sum((matching & earlier[None]).astype(jnp.int32), axis=2)
    source = jnp.arange(owner_count, dtype=jnp.int32)[:, None]
    arrive = (source * slot_count + rank).reshape(-1)
    here = lax.dynamic_slice_in_dim(owners * slot_count + rank, joined_here, 1, 0)[0]
    fills = here[None, :] == jnp.arange(all_slots)[:, None]
    outgoing = jnp.sum(fills * jnp.arange(tiles_dev)[None, :], axis=1)
    local = jnp.arange(tiles_dev, dtype=jnp.int32) + joined_here * tiles_dev
    hits = (listing[None, :] == local[:, None]).astype(jnp.int32)
    slot = jnp.sum(hits * arrive[None, :], axis=1)

    tile_weight = (weight_level[0].astype(jnp.float32) + 1.0) / 8.0
    all_weight = lax.all_gather(tile_weight, "joined", tiled=True)
    weight = jnp.sum(hits.astype(jnp.float32) * all_weight[None, :], axis=1)

    tiles = observed.reshape(tiles_dev, rows, size_x)
    packed = jnp.take(tiles, outgoing, axis=0, mode="clip")
    arrived = lax.all_to_all(
        packed.reshape(owner_count, slot_count, rows, size_x), "joined", 0, 0, tiled=True
    ).reshape(all_slots, rows, size_x)
    current = estimate.reshape(tiles_dev, rows, size_x)
    part = project(slot, plane, line, weight, arrived, current)
    numerator, denominator = lax.psum((part, weight), "view")
    refined = current * (numerator / denominator[:, None, None])
    return refined.reshape(estimate.shape)


def solution(mesh):
    return jax.shard_map(
        shards,
        mesh=mesh,
        in_specs=(
            P("view", "joined", None, None, None),
            P("joined", None, None, None),
            P("view", None, None),
            P(),
            P("view", "joined"),
        ),
        out_specs=P("joined", None, None, None),
        check_vma=False,
    )
```

time: 702 us -> 367 us (0.52)
  waiting for transfers between devices: 453 us -> 135 us
  blocking collectives: 10.1 us -> 154 us
  matrix products: 78.1 us -> 0 us
  other arithmetic: 86.2 us -> 8.45 us
  Pallas kernels: 0 us -> 33.5 us
  local copies, waits for them, and re-layouts: 44.6 us -> 14.6 us
  starting transfers between devices: 14.9 us -> 6.5 us
    all_to_all x3 -> x1, waiting for transfers between devices: 360 us -> 36.2 us  [shards(): lax.all_to_all(packed.reshape(owner_count, slot_count, rows, size_x), 'jo...]
    unnamed x0 -> x1, blocking collectives: none -> 144 us
    dot_general x4 -> x0, matrix products: 78.1 us -> none  [the longest x1 59.2 us: spread(): jnp.einsum('yb,tzyx->tzbx', along_y, volume, precision=lax.Precision.HIGH...]
    div x3 -> x1, other arithmetic: 52.7 us -> 0.07 us  [shards(): kernel_rows = psf_taps[0] / jnp.sum(psf_taps[0], axis=-1, keepdims=True)]
    pallas_call x0 -> x1, Pallas kernels: none -> 33.5 us  [project(): pl.pallas_call(project_kernel, grid_spec=pltpu.PrefetchScalarGridSpec(num...]
    select_n x12 -> x1, other arithmetic: 24.8 us -> 0.01 us  [shards(): owners = (listing // tiles_dev).reshape(owner_count, tiles_dev)]
    gather x6 -> x1, local copies, waits for them, and re-layouts: 26.9 us -> 6.48 us  [shards(): packed = jnp.take(tiles, outgoing, axis=0, mode='clip')]
    all_to_all x2 -> x0, local copies, waits for them, and re-layouts: 11 us -> none  [the longest x1 10.5 us: shards(): lax.all_to_all(pack(weighted, returning), 'joined', split_axis=0, concat_...]
  transfers between devices with their start and end apart: 4 -> 2, of which waited for: 3 -> 2; matrix products, arithmetic and copies ran while one was open for 23% -> 1% of each run, Pallas kernels for 0% -> 0%
where the time goes in v1:
time: 367 us; the launch traced here: 366 us
  blocking collectives  154 us (42%)
  waiting for transfers between devices  135 us (37%)
  Pallas kernels  33.5 us (9%)
  local copies, waits for them, and re-layouts  14.6 us (4%)
  between operations  14.2 us (4%)
  other arithmetic  8.45 us (2%)
  starting transfers between devices  6.5 us (2%)
    unnamed x1, blocking collectives  144 us
    psum x1, waiting for transfers between devices, shards(): numerator, denominator = lax.psum((part, weight), 'view')  99.1 us
    all_to_all x1, waiting for transfers between devices, shards(): lax.all_to_all(packed.reshape(owner_count, slot_count, rows, size_x), 'jo...  36.2 us
    pallas_call x1, Pallas kernels, project(): pl.pallas_call(project_kernel, grid_spec=pltpu.PrefetchScalarGridSpec(num...  33.5 us
    psum x1, blocking collectives, shards(): numerator, denominator = lax.psum((part, weight), 'view')  9.92 us
  transfers between devices with their start and end apart: 2, of which 2 were waited for; matrix products, arithmetic and copies ran while one was open for 1% of the time, Pallas kernels for 0%

profile of v1, /device:TPU:0, one launch (start us, length us, event | category | flops | bytes accessed | tf_op | source)
XLA Modules:
  0.0 366.4 jit_solution(2477387505930220230)
XLA Ops:
  6.5 0.5 broadcast.155
  7.1 1.4 fusion.6
  8.4 0.1 squeeze.9
  8.5 0.3 convert_reduce_fusion
  8.8 0.1 multiply_add_fusion
  8.9 0.1 select_reduce_fusion.3
  9.0 6.5 %gather_fusion = f32[64,256,128]{2,1,0:T(8,128)} fusion(f32[32,256,128]{2,1,0:T(8,128)} %bitcast.30, s32[1024]{0:T(1024)S(1)} %pad_clamp_fusion), kind=kCustom, calls=%fused_computation | custom fusion | bytes 16777472 | tf_op jit(solution)/shard_map/jit(_take)/gather | solution.py:95
  15.5 6.5 %all-to-all-start = ((f32[8,8,256,128]{3,2,1,0:T(8,128)}), f32[8,8,256,128]{3,2,1,0:T(8,128)}, u32[]{:S(2)}, u32[]{:S(2)}) async-start(f32[8,8,256,128]{3,2,1,0:T(8,128)} %bitcast.29), calls=%async_computation | async-start | bytes 16777216 | tf_op jit(solution)/shard_map/all_to_all | solution.py:96
  21.9 0.0 all-reduce.3.cloned.1.call-start
  22.0 0.1 add.81
  22.1 0.1 reduce_sum.74
  22.2 0.1 bitcast_divide_fusion
  22.3 0.2 select_reduce_fusion.2
  22.5 0.1 copy.8
  22.6 0.1 copy.9
  22.7 0.2 broadcast_multiply_fusion
  22.9 0.9 mul.104
  23.8 0.1 copy.11.plane_ref
  24.0 0.3 select_reduce_fusion.line_ref
  24.2 0.1 copy.10
  24.3 0.6 dynamic-slice
  25.6 0.1 bitcast_dynamic-update-slice_fusion
  25.7 143.8 %all-reduce = f32[256]{0:T(256)S(1)} all-reduce(f32[256]{0:T(256)S(1)} %bitcast_dynamic-update-slice_fusion), channel_id=2, replica_groups=mesh['view'=4,'joined'=8] {'joined'}, use_global_device_ids=true, to_apply=%add | all-reduce | flops 256 | bytes 2048
  169.5 0.2 fusion.slot_ref
  169.7 0.2 fusion.3.weight_ref
  169.9 36.2 %all-to-all-done = f32[8,8,256,128]{3,2,1,0:T(8,128)} async-done(((f32[8,8,256,128]{3,2,1,0:T(8,128)}), f32[8,8,256,128]{3,2,1,0:T(8,128)}, u32[]{:S(2)}, u32[]{:S(2)}) %all-to-all-start) | async-done | bytes 8388640 | tf_op jit(solution)/shard_map/all_to_all | solution.py:96
  206.1 2.2 copy-done
  208.3 33.5 %shard_map.55 = f32[32,256,128]{2,1,0:T(8,128)S(1)} custom-call(s32[32]{0:T(128)S(1)} %fusion.slot_ref, f32[256,256]{1,0:T(8,128)S(1)} %copy.11.plane_ref, f32[256,256]{1,0:T(8,128)S(1)} %bitcast.27, f32[128,128]{1,0:T(8,128)S(1)} %select_reduce_fusion.line_ref, f32[128,128]{1,0:T(8,128)S(1)} %bitcast.28, f32[32]{0:T(128)S(1)} %fusion.3.weight_ref, ...), custom_call_target="tpu_custom_call" | custom-call | tf_op jit(solution)/shard_map/pallas_call | solution.py:41
  241.8 2.0 copy-done.1
  243.9 9.9 %psum.15 = f32[32]{0:T(128)S(1)} all-reduce(f32[32]{0:T(128)S(1)} %fusion.3.weight_ref), channel_id=1, replica_groups=mesh['view'=4,'joined'=8] {'view'}, use_global_device_ids=true, to_apply=%region_9.10 | all-reduce | flops 32 | bytes 256 | tf_op jit(solution)/shard_map/psum | solution.py:101
  253.8 99.1 %all-reduce.3.cloned.1.call-done = f32[32,256,128]{2,1,0:T(8,128)} async-done(((f32[32,256,128]{2,1,0:T(8,128)}), f32[32,256,128]{2,1,0:T(8,128)}) %all-reduce.3.cloned.1.call-update) | async-done | bytes 4194320 | tf_op jit(solution)/shard_map/psum | solution.py:101
  352.9 6.6 %divide_multiply_fusion = f32[32,256,128]{2,1,0:T(8,128)} fusion(f32[32,256,128]{2,1,0:T(8,128)} %all-reduce.3.cloned.1.call-done, f32[32]{0:T(128)S(1)} %psum.15, f32[32,16,16,128]{3,2,1,0:T(8,128)} %param.6), kind=kLoop, calls=%fused_computation.1 | loop fusion | flops 2097152 | bytes 12583040 | tf_op jit(solution)/shard_map/mul | solution.py:102
  (19 shorter events, 0.1 us)
Async XLA Ops:
  15.5 6.6 %copy-start.2 = (f32[1,3,31]{2,0,1:T(1,128)S(1)}, f32[1,3,31]{2,0,1:T(1,128)}, u32[]{:S(2)}) copy-start(f32[1,3,31]{2,0,1:T(1,128)} %param.7) | copy-start | bytes 1120
  15.5 190.6 %all-to-all-start = ((f32[8,8,256,128]{3,2,1,0:T(8,128)}), f32[8,8,256,128]{3,2,1,0:T(8,128)}, u32[]{:S(2)}, u32[]{:S(2)}) async-start(f32[8,8,256,128]{3,2,1,0:T(8,128)} %bitcast.29), calls=%async_computation | async-start | bytes 16777216 | tf_op jit(solution)/shard_map/all_to_all | solution.py:96
  21.9 2.4 copy-start.4
  21.9 3.6 copy-start.3
  21.9 331.0 %all-reduce.3.cloned.1.call-start = ((), (), s32[]{:S(2)}) async-start(), calls=%async_computation.1 | async-start | bytes 8388608 | tf_op jit(solution)/shard_map/psum | solution.py:101
  206.1 2.2 copy-start
  241.8 2.0 copy-start.1
Sparse Core Ops, SparseCore 0:
  244.0 108.8 all-reduce.2

commit v2 on v1

v2 whole, which is shorter than its diff:
```python
import functools

import jax
import jax.numpy as jnp
from jax import lax
from jax.experimental import pallas as pl
from jax.experimental.pallas import tpu as pltpu
from jax.sharding import PartitionSpec as P

PARTS = (80, 80, 64, 32)
PIECES = len(PARTS)
STARTS = tuple(sum(PARTS[:p]) for p in range(PIECES))
MESH = pl.DeviceIdType.MESH


def bands(rows, extent):
    taps = rows.shape[-1]
    offset = jnp.arange(extent)[None, :] - jnp.arange(extent)[:, None] + taps // 2
    chosen = (offset[:, :, None] == jnp.arange(taps)[None, None, :]).astype(jnp.float32)
    return jnp.sum(chosen * rows, axis=-1)


def split(value):
    high = value.astype(jnp.bfloat16)
    low = (value - high.astype(jnp.float32)).astype(jnp.bfloat16)
    return high, low


def matmul(a, b):
    dot = functools.partial(jnp.dot, preferred_element_type=jnp.float32)
    return dot(a[0], b[0]) + (dot(a[0], b[1]) + dot(a[1], b[0]))


def kernel(
    views, owners, slots,
    outgoing, slot_weight, slot, planes, lines, seen, current, own_weight, out, weight_out, *scratch,
):
    sends, arrived, regroup = scratch[:PIECES], scratch[PIECES : 2 * PIECES], scratch[2 * PIECES : 3 * PIECES]
    (ratio_in, blurred, total, plane_all, line_all, plane_high, plane_low, line_high, line_low,
     z_send, z_recv, xy_send, xy_recv, m_send, m_recv, g_send, g_recv, own_sem,
     weight_all, w_send, w_recv, v_send, v_recv, w_sem) = scratch[3 * PIECES :]
    share, rows, lanes = current.shape
    here, view = lax.axis_index("joined"), lax.axis_index("view")
    owner_at = lambda d: lax.rem(here + d, owners)
    view_at = lambda u: lax.rem(view + u, views)
    sides = (view + 1 - 2 * lax.rem(view, 2), lax.rem(view + 2, 4))

    barrier = pltpu.get_barrier_semaphore()
    for d in range(1, owners):
        pl.semaphore_signal(barrier, inc=1, device_id={"joined": owner_at(d)}, device_id_type=MESH)
    for u in range(1, views):
        pl.semaphore_signal(barrier, inc=1, device_id={"view": view_at(u)}, device_id_type=MESH)
    pl.semaphore_wait(barrier, owners + views - 2)

    def matrix_copies(u):
        return [
            pltpu.make_async_remote_copy(
                src_ref=src, dst_ref=dst.at[view],
                send_sem=m_send.at[i, u - 1], recv_sem=m_recv.at[i, u - 1],
                device_id={"view": view_at(u)}, device_id_type=MESH,
            )
            for i, (src, dst) in enumerate(((planes, plane_all), (lines, line_all)))
        ]

    def z_copy(p, d):
        return pltpu.make_async_remote_copy(
            src_ref=sends[p].at[d - 1],
            dst_ref=arrived[p].at[pl.ds(here * slots, slots)],
            send_sem=z_send.at[p, d - 1], recv_sem=z_recv.at[p, d - 1],
            device_id={"joined": owner_at(d)}, device_id_type=MESH,
        )

    def xy_copy(p, u):
        return pltpu.make_async_remote_copy(
            src_ref=regroup[p].at[u - 1],
            dst_ref=ratio_in.at[view, :, pl.ds(STARTS[p], PARTS[p])],
            send_sem=xy_send.at[p, u - 1], recv_sem=xy_recv.at[p, u - 1],
            device_id={"view": view_at(u)}, device_id_type=MESH,
        )

    def gather_copy(k, side):
        return pltpu.make_async_remote_copy(
            src_ref=total.at[k], dst_ref=out.at[view, k],
            send_sem=g_send.at[k, side], recv_sem=g_recv.at[k, side],
            device_id={"view": sides[side]}, device_id_type=MESH,
        )

    def forward_copy(k, side):
        place = out.at[sides[side], k]
        return pltpu.make_async_remote_copy(
            src_ref=place, dst_ref=place,
            send_sem=g_send.at[k, 2], recv_sem=g_recv.at[k, 2],
            device_id={"view": sides[1 - side]}, device_id_type=MESH,
        )

    def weight_copy(d):
        return pltpu.make_async_remote_copy(
            src_ref=own_weight, dst_ref=weight_all.at[here],
            send_sem=w_send.at[d - 1], recv_sem=w_recv.at[d - 1],
            device_id={"joined": owner_at(d)}, device_id_type=MESH,
        )

    def weights_copy(u):
        return pltpu.make_async_remote_copy(
            src_ref=weight_all, dst_ref=weight_out.at[view],
            send_sem=v_send.at[u - 1], recv_sem=v_recv.at[u - 1],
            device_id={"view": view_at(u)}, device_id_type=MESH,
        )

    def own_copy(k):
        return pltpu.make_async_copy(total.at[k], out.at[view, k], own_sem.at[k])

    def pack(p):
        window = pl.ds(STARTS[p], PARTS[p])
        for d in list(range(1, owners)) + [0]:

            def fill(s, carry):
                at = owner_at(d) * slots + s
                piece = seen[outgoing[at], window] * slot_weight[at]
                if d == 0:
                    arrived[p][here * slots + s] = piece
                else:
                    sends[p][d - 1, s] = piece
                return carry

            lax.fori_loop(0, slots, fill, 0)
            if d:
                z_copy(p, d).start()

    def regroup_piece(p):
        for d in range(1, owners):
            z_copy(p, d).wait_recv()
        for u in list(range(1, views)) + [0]:

            def move(k, carry):
                piece = arrived[p][slot[view_at(u) * share + k]]
                if u == 0:
                    ratio_in[view, k, pl.ds(STARTS[p], PARTS[p])] = piece
                else:
                    regroup[p][u - 1, k] = piece
                return carry

            lax.fori_loop(0, share, move, 0)
            if u:
                xy_copy(p, u).start()

    own_weights = pltpu.make_async_copy(weight_all, weight_out.at[view], w_sem)
    pack(0)
    weight_all[here] = own_weight[...]
    for d in range(1, owners):
        weight_copy(d).start()
    plane_all[view] = planes[...]
    line_all[view] = lines[...]
    for u in range(1, views):
        for copy in matrix_copies(u):
            copy.start()
    pack(1)
    for u in range(1, views):
        for copy in matrix_copies(u):
            copy.wait_recv()

    def prepare(v, carry):
        for i in range(2):
            plane_high[v, i], plane_low[v, i] = split(plane_all[v, i])
            line_high[v, i], line_low[v, i] = split(line_all[v, i])

        def blur_one(k, inner):
            half = matmul(split(current[k]), (line_high[v, 1], line_low[v, 1]))
            blurred[v, k] = matmul((plane_high[v, 0], plane_low[v, 0]), split(half))
            return inner

        return lax.fori_loop(0, share, blur_one, carry)

    lax.fori_loop(0, views, prepare, 0)

    for p in range(PIECES):
        regroup_piece(p)
        if p == 0:
            for d in range(1, owners):
                weight_copy(d).wait_recv()
            for u in range(1, views):
                weights_copy(u).start()
            own_weights.start()
        if p + 2 < PIECES:
            pack(p + 2)
    for p in range(PIECES):
        for u in range(1, views):
            xy_copy(p, u).wait_recv()

    def finish_one(k):
        def back(v, inner):
            ratio = ratio_in[v, k] / blurred[v, k]
            half = matmul(split(ratio), (line_high[v, 0], line_low[v, 0]))
            return inner + matmul((plane_high[v, 1], plane_low[v, 1]), split(half))

        total[k] = lax.fori_loop(0, views, back, jnp.zeros((rows, lanes), jnp.float32))
        for side in range(2):
            gather_copy(k, side).start()
        own_copy(k).start()

    def forward_pair(pair):
        for side in range(2):
            gather_copy(2 * pair + side, side).wait_recv()
            forward_copy(2 * pair + side, side).start()

    def finish(pair, carry):
        finish_one(2 * pair)
        finish_one(2 * pair + 1)

        @pl.when(pair > 0)
        def _():
            forward_pair(pair - 1)

        return carry

    lax.fori_loop(0, share // 2, finish, 0)
    forward_pair(share // 2 - 1)

    for u in range(1, views):
        for copy in matrix_copies(u):
            copy.wait_send()
    for p in range(PIECES):
        for d in range(1, owners):
            z_copy(p, d).wait_send()
        for u in range(1, views):
            xy_copy(p, u).wait_send()

    for d in range(1, owners):
        weight_copy(d).wait_send()
    for u in range(1, views):
        weights_copy(u).wait()
    own_weights.wait()

    def drain(pair, carry):
        for side in range(2):
            k = 2 * pair + side
            own_copy(k).wait()
            gather_copy(k, side).wait_send()
            gather_copy(k, 1 - side).wait()
            forward_copy(k, side).wait()
        return carry

    lax.fori_loop(0, share // 2, drain, 0)


def exchange(views, owners, slots, outgoing, slot_weight, slot, planes, lines, seen, current, weight):
    share, rows, lanes = current.shape
    f32, bf16 = jnp.float32, jnp.bfloat16
    dma = pltpu.SemaphoreType.DMA
    smem, vmem = pl.BlockSpec(memory_space=pltpu.SMEM), pl.BlockSpec(memory_space=pltpu.VMEM)
    scratch = (
        [pltpu.VMEM((owners - 1, slots, part, lanes), f32) for part in PARTS]
        + [pltpu.VMEM((owners * slots, part, lanes), f32) for part in PARTS]
        + [pltpu.VMEM((views - 1, share, part, lanes), f32) for part in PARTS]
        + [pltpu.VMEM((views, share, rows, lanes), f32)] * 2
        + [pltpu.VMEM((share, rows, lanes), f32)]
        + [pltpu.VMEM((views,) + planes.shape, f32), pltpu.VMEM((views,) + lines.shape, f32)]
        + [pltpu.VMEM((views,) + planes.shape, bf16)] * 2
        + [pltpu.VMEM((views,) + lines.shape, bf16)] * 2
        + [dma((PIECES, owners - 1))] * 2
        + [dma((PIECES, views - 1))] * 2
        + [dma((2, views - 1))] * 2
        + [dma((share, 3))] * 2
        + [dma((share,))]
        + [pltpu.VMEM((owners,) + weight.shape, f32)]
        + [dma((owners - 1,))] * 2
        + [dma((views - 1,))] * 2
        + [dma(())]
    )
    return pl.pallas_call(
        functools.partial(kernel, views, owners, slots),
        out_shape=(
            jax.ShapeDtypeStruct((views, share, rows, lanes), f32),
            jax.ShapeDtypeStruct((views, owners) + weight.shape, f32),
        ),
        in_specs=[smem] * 3 + [vmem] * 5,
        out_specs=[pl.BlockSpec(memory_space=pl.ANY)] * 2,
        scratch_shapes=scratch,
        compiler_params=pltpu.CompilerParams(
            collective_id=0, has_side_effects=True, vmem_limit_bytes=56 * 1024 * 1024
        ),
        cost_estimate=pl.CostEstimate(
            flops=6 * 2 * views * share * 2 * rows * lanes * (rows + lanes) // 2,
            bytes_accessed=4 * (seen.size + 5 * current.size),
            transcendentals=0,
        ),
    )(outgoing, slot_weight, slot, planes, lines, seen, current, weight)


def shards(observed, estimate, psf_taps, tile_block, weight_level):
    owners, views = lax.axis_size("joined"), lax.axis_size("view")
    view_here, joined_here = lax.axis_index("view"), lax.axis_index("joined")
    tiles_dev, size_z, size_y, size_x = estimate.shape
    rows = size_z * size_y
    slots = 2 * tiles_dev // owners
    all_slots = owners * slots
    share = tiles_dev // views

    kernel_rows = psf_taps[0] / jnp.sum(psf_taps[0], axis=-1, keepdims=True)
    along_z = bands(kernel_rows[0], size_z)
    along_y = bands(kernel_rows[1], size_y)
    line = bands(kernel_rows[2], size_x)
    plane = (along_z[:, None, :, None] * along_y[None, :, None, :]).reshape(rows, rows)

    listing = lax.dynamic_index_in_dim(tile_block, view_here, 0, keepdims=False)
    owner_of = (listing // tiles_dev).reshape(owners, tiles_dev)
    earlier = jnp.arange(tiles_dev)[None, :] < jnp.arange(tiles_dev)[:, None]
    matching = owner_of[:, :, None] == owner_of[:, None, :]
    rank = jnp.sum((matching & earlier[None]).astype(jnp.int32), axis=2)
    source = jnp.arange(owners, dtype=jnp.int32)[:, None]
    arrive = (source * slots + rank).reshape(-1)
    here = lax.dynamic_slice_in_dim(owner_of * slots + rank, joined_here, 1, 0)[0]
    fills = (here[None, :] == jnp.arange(all_slots)[:, None]).astype(jnp.int32)
    outgoing = jnp.sum(fills * jnp.arange(tiles_dev, dtype=jnp.int32)[None, :], axis=1)
    local = jnp.arange(tiles_dev, dtype=jnp.int32) + joined_here * tiles_dev
    hits = (tile_block[:, None, :] == local[None, :, None]).astype(jnp.int32)
    hits_here = lax.dynamic_index_in_dim(hits, view_here, 0, keepdims=False)
    slot = jnp.sum(hits_here * arrive[None, :], axis=1)

    tile_weight = (weight_level[0].astype(jnp.float32) + 1.0) / 8.0
    slot_weight = jnp.sum(fills.astype(jnp.float32) * tile_weight[None, :], axis=1)
    current = estimate.reshape(tiles_dev, rows, size_x)
    mine = lax.dynamic_slice_in_dim(current, view_here * share, share, 0)
    weight_row = jnp.broadcast_to(jnp.pad(tile_weight, (0, -tiles_dev % 128)), (8, 128))
    numerator, all_weight = exchange(
        views, owners, slots,
        outgoing, slot_weight, slot,
        jnp.stack([plane, plane.T]), jnp.stack([line, line.T]),
        observed.reshape(tiles_dev, rows, size_x), mine, weight_row,
    )
    numerator = numerator.reshape(tiles_dev, rows, size_x)
    all_weight = all_weight[:, :, 0, :tiles_dev].reshape(views, 1, -1)
    denominator = jnp.sum(hits.astype(jnp.float32) * all_weight, axis=(0, 2))
    refined = current * (numerator / denominator[:, None, None])
    return refined.reshape(estimate.shape)


def solution(mesh):
    return jax.shard_map(
        shards,
        mesh=mesh,
        in_specs=(
            P("view", "joined", None, None, None),
            P("joined", None, None, None),
            P("view", None, None),
            P(),
            P("view", "joined"),
        ),
        out_specs=P("joined", None, None, None),
        check_vma=False,
    )
```

time: 367 us -> 255 us (0.69)
  Pallas kernels: 33.5 us -> 230 us
  blocking collectives: 154 us -> 0 us
  waiting for transfers between devices: 135 us -> 0 us
  between operations: 14.2 us -> 0.08 us
  local copies, waits for them, and re-layouts: 14.6 us -> 7.01 us
  starting transfers between devices: 6.5 us -> 0 us
  other arithmetic: 8.45 us -> 14.2 us
    pallas_call x1, Pallas kernels: 33.5 us -> 230 us  [exchange(): pl.pallas_call(functools.partial(kernel, views, owners, slots), out_shape...]
    unnamed x1 -> x0, blocking collectives: 144 us -> none
    psum x1 -> x0, waiting for transfers between devices: 99.1 us -> none  [shards(): numerator, denominator = lax.psum((part, weight), 'view')]
    all_to_all x1 -> x0, waiting for transfers between devices: 36.2 us -> none  [shards(): lax.all_to_all(packed.reshape(owner_count, slot_count, rows, size_x), 'jo...]
    psum x1 -> x0, blocking collectives: 9.92 us -> none  [shards(): numerator, denominator = lax.psum((part, weight), 'view')]
    gather x1 -> x0, local copies, waits for them, and re-layouts: 6.48 us -> none  [shards(): packed = jnp.take(tiles, outgoing, axis=0, mode='clip')]
    all_to_all x1 -> x0, starting transfers between devices: 6.46 us -> none  [shards(): lax.all_to_all(packed.reshape(owner_count, slot_count, rows, size_x), 'jo...]
    unnamed x12 -> x2, local copies, waits for them, and re-layouts: 4.8 us -> 0.01 us
  transfers between devices with their start and end apart: 2 -> 0, of which waited for: 2 -> 0; matrix products, arithmetic and copies ran while one was open for 1% -> 0% of each run, Pallas kernels for 0% -> 0%
where the time goes in v2:
time: 255 us; the launch traced here: 252 us
  Pallas kernels  230 us (90%)
  other arithmetic  14.2 us (6%)
  local copies, waits for them, and re-layouts  7.01 us (3%)
    pallas_call x1, Pallas kernels, exchange(): pl.pallas_call(functools.partial(kernel, views, owners, slots), out_shape...  230 us
    mul x1, other arithmetic, shards(): refined = current * (numerator / denominator[:, None, None])  6.6 us

profile of v2, /device:TPU:0, one launch (start us, length us, event | category | flops | bytes accessed | tf_op | source)
XLA Modules:
  0.0 251.7 jit_solution(12872394732469575825)
XLA Ops:
  0.0 0.7 multiply_bitcast_fusion
  0.7 0.8 reduce_sum.85
  1.5 0.7 dynamic-slice_reduce_fusion
  2.2 0.8 bitcast_divide_fusion
  2.9 0.1 squeeze.13
  3.0 0.6 broadcast_in_dim.2.own_weight
  3.6 0.3 convert_reduce_fusion
  3.9 0.1 broadcast_add_fusion
  4.0 0.1 add.89
  4.1 0.6 multiply_reduce_fusion.1.slot_weight
  4.7 0.7 select_reduce_fusion.3.outgoing
  5.3 0.2 select_reduce_fusion.2
  5.6 0.1 copy.8
  5.6 0.1 copy.9
  5.7 0.3 select_reduce_fusion
  6.0 0.1 copy.11
  6.1 0.7 pad_maximum_fusion.1.lines
  6.8 0.8 compare_convert_fusion
  7.5 0.6 fusion.slot
  8.2 2.3 constant_dynamic-slice_fusion.current
  10.4 0.2 broadcast_multiply_fusion
  10.6 0.9 mul.138
  11.6 0.9 reshape.171
  12.5 0.1 copy.12
  12.6 0.8 pad_maximum_fusion.planes
  13.5 0.0 copy-start
  13.5 230.4 %shard_map.55 = (f32[4,8,256,128]{3,2,1,0:T(8,128)}, f32[4,8,8,128]{3,2,1,0:T(8,128)}) custom-call(s32[64]{0:T(128)} %select_reduce_fusion.3.outgoing, f32[64]{0:T(128)} %multiply_reduce_fusion.1.slot_weight, s32[32]{0:T(128)} %fusion.slot, f32[2,256,256]{2,1,0:T(8,128)} %pad_maximum_fusion.planes, f32[2,128,128]{2,1,0:T(8,128)} %pad_maximum_fusion.1.lines, ...), custom_call_target="tpu_custom_call" | custom-call | flops 4831838208 | bytes 9437184 | tf_op jit(solution)/shard_map/pallas_call | solution.py:270
  243.8 0.9 slice_reduce_fusion
  244.8 0.1 mul.143
  244.9 0.0 copy-done
  244.9 0.2 multiply_reduce_fusion
  245.1 6.6 %divide_multiply_fusion = f32[32,16,16,128]{3,2,1,0:T(8,128)} fusion(f32[32,16,16,128]{3,2,1,0:T(8,128)} %param.6, f32[32,16,16,128]{3,2,1,0:T(8,128)} %bitcast.35, f32[32]{0:T(128)S(1)} %multiply_reduce_fusion), kind=kLoop, calls=%fused_computation | loop fusion | flops 2097152 | bytes 12583040 | tf_op jit(solution)/shard_map/mul | solution.py:334
  (9 shorter events, 0.1 us)
Async XLA Ops:
  13.5 231.4 %copy-start = (s32[4,256]{1,0:T(4,128)S(1)}, s32[4,256]{1,0:T(4,128)}, u32[]{:S(2)}) copy-start(s32[4,256]{1,0:T(4,128)} %param.8) | copy-start | bytes 12292

commit v3 on v2

--- a/solution.py
+++ b/solution.py
@@ -7,7 +7,7 @@
 from jax.experimental.pallas import tpu as pltpu
 from jax.sharding import PartitionSpec as P
 
-PARTS = (80, 80, 64, 32)
+PARTS = (96, 88, 56, 16)
 PIECES = len(PARTS)
 STARTS = tuple(sum(PARTS[:p]) for p in range(PIECES))
 MESH = pl.DeviceIdType.MESH
@@ -193,7 +193,9 @@
             half = matmul(split(ratio), (line_high[v, 0], line_low[v, 0]))
             return inner + matmul((plane_high[v, 1], plane_low[v, 1]), split(half))
 
-        total[k] = lax.fori_loop(0, views, back, jnp.zeros((rows, lanes), jnp.float32))
+        total[k] = lax.fori_loop(
+            0, views, back, jnp.zeros((rows, lanes), jnp.float32), unroll=True
+        )
         for side in range(2):
             gather_copy(k, side).start()
         own_copy(k).start()

time: 255 us -> 254 us (level)
  no operation moved by 1% of the time
where the time goes in v3:
time: 254 us; the launch traced here: 253 us
  Pallas kernels  232 us (91%)
  other arithmetic  14.2 us (6%)
  local copies, waits for them, and re-layouts  7.01 us (3%)
    pallas_call x1, Pallas kernels, exchange(): pl.pallas_call(functools.partial(kernel, views, owners, slots), out_shape...  232 us
    mul x1, other arithmetic, shards(): refined = current * (numerator / denominator[:, None, None])  6.6 us

profile of v3, /device:TPU:0, one launch (start us, length us, event | category | flops | bytes accessed | tf_op | source)
XLA Modules:
  0.0 252.9 jit_solution(15487441641386540813)
XLA Ops:
  0.0 0.7 multiply_bitcast_fusion
  0.7 0.8 reduce_sum.85
  1.5 0.7 dynamic-slice_reduce_fusion
  2.2 0.8 bitcast_divide_fusion
  2.9 0.1 squeeze.13
  3.0 0.6 broadcast_in_dim.2.own_weight
  3.6 0.3 convert_reduce_fusion
  3.9 0.1 broadcast_add_fusion
  4.0 0.1 add.89
  4.1 0.6 multiply_reduce_fusion.1.slot_weight
  4.7 0.7 select_reduce_fusion.3.outgoing
  5.3 0.2 select_reduce_fusion.2
  5.6 0.1 copy.8
  5.6 0.1 copy.9
  5.7 0.3 select_reduce_fusion
  6.0 0.1 copy.11
  6.1 0.7 pad_maximum_fusion.1.lines
  6.8 0.8 compare_convert_fusion
  7.5 0.6 fusion.slot
  8.2 2.3 constant_dynamic-slice_fusion.current
  10.4 0.2 broadcast_multiply_fusion
  10.6 0.9 mul.138
  11.6 0.9 reshape.171
  12.5 0.1 copy.12
  12.6 0.8 pad_maximum_fusion.planes
  13.5 0.0 copy-start
  13.5 231.6 %shard_map.55 = (f32[4,8,256,128]{3,2,1,0:T(8,128)}, f32[4,8,8,128]{3,2,1,0:T(8,128)}) custom-call(s32[64]{0:T(128)} %select_reduce_fusion.3.outgoing, f32[64]{0:T(128)} %multiply_reduce_fusion.1.slot_weight, s32[32]{0:T(128)} %fusion.slot, f32[2,256,256]{2,1,0:T(8,128)} %pad_maximum_fusion.planes, f32[2,128,128]{2,1,0:T(8,128)} %pad_maximum_fusion.1.lines, ...), custom_call_target="tpu_custom_call" | custom-call | flops 4831838208 | bytes 9437184 | tf_op jit(solution)/shard_map/pallas_call | solution.py:272
  245.1 0.9 slice_reduce_fusion
  246.0 0.1 mul.143
  246.1 0.0 copy-done
  246.1 0.2 multiply_reduce_fusion
  246.3 6.6 %divide_multiply_fusion = f32[32,16,16,128]{3,2,1,0:T(8,128)} fusion(f32[32,16,16,128]{3,2,1,0:T(8,128)} %param.6, f32[32,16,16,128]{3,2,1,0:T(8,128)} %bitcast.35, f32[32]{0:T(128)S(1)} %multiply_reduce_fusion), kind=kLoop, calls=%fused_computation | loop fusion | flops 2097152 | bytes 12583040 | tf_op jit(solution)/shard_map/mul | solution.py:336
  (9 shorter events, 0.1 us)
Async XLA Ops:
  13.5 232.6 %copy-start = (s32[4,256]{1,0:T(4,128)S(1)}, s32[4,256]{1,0:T(4,128)}, u32[]{:S(2)}) copy-start(s32[4,256]{1,0:T(4,128)} %param.8) | copy-start | bytes 12292
